TPU v7x, 32 devices: a whole 2x2x4 slice. The times are simulated.
32 devices in a mesh: gx: 2 (over core), gy: 4 (over y, x), gz: 4 (over z).
Axes of the slice: x: 2, y: 2, z: 4, core: 2. Of those that a mesh axis runs over, the one named last changes fastest.
Arguments:
- resid_x: float32 [6, 8, 4, 120, 512], P('gx', 'gy', 'gz'), may hold values from -6 to 6
- resid_y: float32 [4, 12, 4, 120, 512], P('gx', 'gy', 'gz'), may hold values from -6 to 6
- face_weights: float32 [4, 8, 4, 4, 120], P('gx', 'gy', 'gz'), may hold values from 0.25 to 0.75
- face_counts: int32 [4, 8, 4, 4], P('gx', 'gy', 'gz'), may hold values from 1 to 4, as said below
- neumann: bfloat16 [4, 8, 4, 480, 480], P('gx', 'gy', 'gz'), may hold values from -0.25 to 0.25
- schur: bfloat16 [4, 8, 4, 480, 480], P('gx', 'gy', 'gz'), may hold values from -0.25 to 0.25
- basis: bfloat16 [4, 8, 4, 480, 64], P('gx', 'gy', 'gz'), may hold values from -0.25 to 0.25
- coarse_map: int32 [4, 8, 4, 64], P('gx', 'gy', 'gz'), may hold values from 0 to 511
- column_inverse: float32 [2, 4, 512, 512], P('gx', 'gy', 'gz'), may hold values from -0.25 to 0.25
- column_basis: float32 [2, 4, 512, 512], P('gx', 'gy', 'gz'), may hold values from -0.25 to 0.25
- top_inverse: float32 [512, 512], replicated, may hold values from -0.09375 to 0.09375
Outputs:
- z_x: float32 [6, 8, 4, 120, 512], P('gx', 'gy', 'gz')
- z_y: float32 [4, 12, 4, 120, 512], P('gx', 'gy', 'gz')
- schur_image: bfloat16 [4, 8, 4, 480, 512], P('gx', 'gy', 'gz')
Inputs may be any that keep to these rules, and one draw needn't show every extreme that they name: `face_counts`: only the first 30 * count of a face's 120 dofs are live; about one face in eight has 4 live mesh faces. `coarse_map`: several local coarse dofs may share a column coarse dof.
All inputs are finite; a program needn't handle non-finite values.
Results may differ from a plain program's by a relative error of at most 0.0063.
Values sent between devices are 32-bit elements; how exact they have to be, the bound alone decides.
A program may use at most 64 MiB of HBM per device.

v0:
```python
import jax
import jax.numpy as jnp
from jax import lax
from jax.sharding import PartitionSpec as P

BLK = 30


def with_halo(array, sides, width):
    for axis, dim in sides:
        size, length = (lax.axis_size(axis), array.shape[dim])
        up = [(i, (i + 1) % size) for i in range(size)]
        down = [(j, i) for i, j in up]
        last = lax.slice_in_dim(array, length - width, length, axis=dim)
        initial = lax.slice_in_dim(array, 0, width, axis=dim)
        before = lax.ppermute(last, axis, up)
        after = lax.ppermute(initial, axis, down)
        array = jnp.concatenate([before, array, after], axis=dim)
    return array


def assemble_x(copies):
    padded = with_halo(copies, (("gx", 0),), 1)
    return copies + jnp.stack([padded[0], jnp.zeros_like(padded[0]), padded[4]], 0)


def assemble_y(copies):
    padded = with_halo(copies, (("gy", 1),), 1)
    return copies + jnp.stack([padded[:, 0], jnp.zeros_like(padded[:, 0]), padded[:, 4]], 1)


def gather_faces(along_x, along_y):
    return jnp.stack([along_x[0:2], along_x[1:3], along_y[:, 0:2], along_y[:, 1:3]], 2)


def on_device(
    resid_x,
    resid_y,
    face_weights,
    face_counts,
    neumann,
    schur,
    basis,
    coarse_map,
    column_inverse,
    column_basis,
    top_inverse,
):
    high = lax.Precision.HIGHEST
    face_dofs = resid_x.shape[3]
    loads = resid_x.shape[4]
    inner = neumann.shape[3]
    coarse_local = basis.shape[4]
    column_size = column_inverse.shape[3]
    dof_index = jnp.arange(face_dofs, dtype=jnp.int32)
    live = (dof_index[None, None, None, :] < face_counts[:, :, 0, :, None] * BLK).astype(
        jnp.float32
    )
    scale = face_weights[:, :, 0] * live
    assembled_x = assemble_x(resid_x)[:, :, 0]
    assembled_y = assemble_y(resid_y)[:, :, 0]
    faces = gather_faces(assembled_x, assembled_y)
    upart = (faces * scale[..., None]).reshape(4, inner, loads).astype(jnp.bfloat16)
    neumann_flat = neumann.reshape(4, inner, inner)
    basis_flat = basis.reshape(4, inner, coarse_local)
    wpart = jnp.einsum("snk,skr->snr", neumann_flat, upart, preferred_element_type=jnp.float32)
    gpart = jnp.einsum("snc,snr->scr", basis_flat, upart, preferred_element_type=jnp.float32)
    targets = coarse_map.reshape(4 * coarse_local)
    onehot = (targets[:, None] == jnp.arange(column_size, dtype=jnp.int32)[None, :]).astype(
        jnp.float32
    )
    column_part = lax.dot_general(
        onehot, gpart.reshape(4 * coarse_local, loads), (((0,), (0,)), ((), ())), precision=high
    )
    column_res = lax.psum(column_part, "gz")
    inverse_rows = column_inverse[0, 0]
    basis_rows = column_basis[0, 0]
    row_count = inverse_rows.shape[0]
    row_start = lax.axis_index("gz") * row_count
    own_rows = lax.dynamic_slice_in_dim(column_res, row_start, row_count, 0)
    level_two = jnp.dot(inverse_rows, column_res, precision=high)
    top_part = lax.dot_general(basis_rows, own_rows, (((0,), (0,)), ((), ())), precision=high)
    column_top = lax.psum(top_part, "gz")
    top_res = lax.psum(column_top, ("gx", "gy"))
    level_three = jnp.dot(top_inverse, top_res, precision=high)
    value_rows = level_two + jnp.dot(basis_rows, level_three, precision=high)
    column_vals = lax.all_gather(value_rows, "gz", axis=0, tiled=True)
    coarse_vals = (
        jnp.dot(onehot, column_vals, precision=high)
        .reshape(4, coarse_local, loads)
        .astype(jnp.bfloat16)
    )
    ypart = wpart + jnp.einsum(
        "snc,scr->snr", basis_flat, coarse_vals, preferred_element_type=jnp.float32
    )
    contrib = ypart.reshape(2, 2, 4, face_dofs, loads) * scale[..., None]
    send_x = jnp.stack(
        [contrib[0, :, 0], contrib[0, :, 1] + contrib[1, :, 0], contrib[1, :, 1]], 0
    )[:, :, None]
    send_y = jnp.stack(
        [contrib[:, 0, 2], contrib[:, 0, 3] + contrib[:, 1, 2], contrib[:, 1, 3]], 1
    )[:, :, None]
    z_x = assemble_x(send_x)
    z_y = assemble_y(send_y)
    zfaces = gather_faces(z_x[:, :, 0], z_y[:, :, 0])
    zsub = (zfaces * live[..., None]).reshape(4, inner, loads).astype(jnp.bfloat16)
    image = jnp.einsum(
        "snk,skr->snr", schur.reshape(4, inner, inner), zsub, preferred_element_type=jnp.float32
    )
    return (z_x, z_y, image.astype(jnp.bfloat16).reshape(2, 2, 1, inner, loads))


def solution(mesh):
    return jax.shard_map(
        on_device,
        mesh=mesh,
        in_specs=(
            P("gx", "gy", "gz", None, None),
            P("gx", "gy", "gz", None, None),
            P("gx", "gy", "gz", None, None),
            P("gx", "gy", "gz", None),
            P("gx", "gy", "gz", None, None),
            P("gx", "gy", "gz", None, None),
            P("gx", "gy", "gz", None, None),
            P("gx", "gy", "gz", None),
            P("gx", "gy", "gz", None),
            P("gx", "gy", "gz", None),
            P(),
        ),
        out_specs=(
            P("gx", "gy", "gz", None, None),
            P("gx", "gy", "gz", None, None),
            P("gx", "gy", "gz", None, None),
        ),
        check_vma=False,
    )
```

profile of v0, /device:TPU:0, one launch (start us, length us, event | category | flops | bytes accessed | tf_op | source)
XLA Modules:
  0.0 289.8 jit_solution(7018751224592183778)
XLA Ops:
  7.2 2.4 fusion.25
  9.6 2.9 %collective-permute-start.2 = (f32[2,1,1,120,512]{4,3,1,0,2:T(8,128)}, f32[2,1,1,120,512]{4,3,1,0,2:T(8,128)}, u32[]{:S(2)}, u32[]{:S(2)}) collective-permute-start(f32[2,1,1,120,512]{4,3,1,0,2:T(8,128)} %get-tuple-element.32), channel_id=1, source_target_pairs={{0,4},{4,8},{8,12},{12,0},{1,5},{5,9},{9,13},{13,1},{2,6},{6,10},{... | collective-permute-start | bytes 1474568 | tf_op jit(solution)/shard_map/ppermute | solution.py:16
  18.2 7.7 %collective-permute-done.2 = f32[2,1,1,120,512]{4,3,1,0,2:T(8,128)} collective-permute-done((f32[2,1,1,120,512]{4,3,1,0,2:T(8,128)}, f32[2,1,1,120,512]{4,3,1,0,2:T(8,128)}, u32[]{:S(2)}, u32[]{:S(2)}) %collective-permute-start.2) | collective-permute-done | bytes 491552 | tf_op jit(solution)/shard_map/ppermute | solution.py:16
  25.9 10.0 %collective-permute-done.3 = f32[2,1,1,120,512]{4,3,1,0,2:T(8,128)} collective-permute-done((f32[2,1,1,120,512]{4,3,1,0,2:T(8,128)}, f32[2,1,1,120,512]{4,3,1,0,2:T(8,128)}, u32[]{:S(2)}, u32[]{:S(2)}) %collective-permute-start.3) | collective-permute-done | bytes 491552 | tf_op jit(solution)/shard_map/ppermute | solution.py:17
  35.8 1.5 fusion.3
  38.7 1.5 maximum_add_fusion
  42.9 1.7 fusion.8
  44.7 52.2 %all-reduce.4.cloned.1.call-done = f32[512,512]{1,0:T(8,128)} async-done(((f32[512,512]{1,0:T(8,128)}), f32[512,512]{1,0:T(8,128)}) %all-reduce.4.cloned.1.call-update) | async-done | bytes 1048592 | tf_op jit(solution)/shard_map/psum | solution.py:75
  96.9 3.0 %convolution_bitcast_fusion = f32[512,512]{0,1:T(8,128)} fusion(f32[1,1,128,512]{3,2,1,0:T(8,128)S(1)} %copy-done.10, f32[512,512]{1,0:T(8,128)} %all-reduce.4.cloned.1.call-done, s32[]{:T(128)S(6)} %select_n.3), kind=kOutput, calls=%fused_computation.17 | convolution fusion | flops 402653184 | bytes 1572868 | tf_op jit(solution)/shard_map/dot_general | solution.py:82
  100.0 51.3 %all-reduce.6.cloned.1.call-done = f32[512,512]{0,1:T(8,128)} async-done(((f32[512,512]{0,1:T(8,128)}), f32[512,512]{0,1:T(8,128)}) %all-reduce.6.cloned.1.call-update) | async-done | bytes 1048592 | tf_op jit(solution)/shard_map/psum | solution.py:83
  151.6 3.5 %fusion.11 = f32[512,128]{1,0:T(8,128)} fusion(f32[512,512]{1,0:T(8,128)S(1)} %copy-done.8, f32[1,1,128,512]{3,2,1,0:T(8,128)} %param.19), kind=kOutput, calls=%fused_computation.37 | convolution fusion | flops 402653184 | bytes 1572864 | tf_op jit(solution)/shard_map/dot_general | solution.py:81
  155.0 55.5 %all-reduce.8.cloned.1.call-done = f32[512,512]{0,1:T(8,128)} async-done(((f32[512,512]{0,1:T(8,128)}), f32[512,512]{0,1:T(8,128)}) %all-reduce.8.cloned.1.call-update) | async-done | bytes 1048592 | tf_op jit(solution)/shard_map/psum | solution.py:84
  210.5 3.4 %fusion.26 = f32[512,512]{1,0:T(8,128)S(1)} fusion(f32[512,512]{0,1:T(8,128)} %all-reduce.8.cloned.1.call-done, f32[512,512]{1,0:T(8,128)} %param.21), kind=kOutput, calls=%fused_computation.57 | convolution fusion | flops 1610612736 | bytes 3145728 | tf_op jit(solution)/shard_map/dot_general | solution.py:85
  213.9 1.7 fusion.5
  215.8 29.3 %all-gather.2.cloned.1.call-done = f32[512,512]{0,1:T(8,128)} async-done(((f32[128,512]{0,1:T(8,128)}), f32[512,512]{0,1:T(8,128)}) %all-gather.2.cloned.1.call-update) | async-done | bytes 1048592 | tf_op jit(solution)/shard_map/all_gather | solution.py:87
  245.1 2.0 convolution_convert_fusion
  247.8 1.4 copy-done.3
  249.2 1.3 convolution_add_fusion
  252.7 2.5 collective-permute-start.7
  255.6 1.3 copy.48
  257.0 10.3 %collective-permute-done.6 = f32[2,1,1,120,512]{4,3,0,2,1:T(8,128)S(1)} collective-permute-done((f32[2,1,1,120,512]{4,3,0,2,1:T(8,128)S(1)}, f32[2,1,1,120,512]{4,3,0,2,1:T(8,128)S(1)}, u32[]{:S(2)}, u32[]{:S(2)}) %collective-permute-start.6) | collective-permute-done | bytes 491552 | tf_op jit(solution)/shard_map/ppermute | solution.py:16
  267.3 8.7 %collective-permute-done.7 = f32[2,1,1,120,512]{4,3,0,2,1:T(8,128)S(1)} collective-permute-done((f32[2,1,1,120,512]{4,3,0,2,1:T(8,128)S(1)}, f32[2,1,1,120,512]{4,3,0,2,1:T(8,128)S(1)}, u32[]{:S(2)}, u32[]{:S(2)}) %collective-permute-start.7) | collective-permute-done | bytes 491552 | tf_op jit(solution)/shard_map/ppermute | solution.py:17
  278.6 2.5 fusion.2
  281.2 1.5 fusion.4
  (94 shorter events, 16.8 us)
Async XLA Ops:
  7.2 240.6 %copy-start = (bf16[2,2,1,480,480]{4,3,2,1,0:T(8,128)(2,1)S(1)}, bf16[2,2,1,480,480]{4,3,2,1,0:T(8,128)(2,1)}, u32[]{:S(2)}) copy-start(bf16[2,2,1,480,480]{4,3,2,1,0:T(8,128)(2,1)} %param.15) | copy-start | bytes 5529604
  7.2 6.3 %copy-start.5 = (f32[3,2,1,120,512]{4,3,2,1,0:T(8,128)S(1)}, f32[3,2,1,120,512]{4,3,2,1,0:T(8,128)}, u32[]{:S(2)}) copy-start(f32[3,2,1,120,512]{4,3,2,1,0:T(8,128)} %param.11) | copy-start | bytes 4423684
  7.2 89.7 %all-reduce.4.cloned.1.call-start = ((), (), s32[]{:S(2)}) async-start(), calls=%async_computation | async-start | bytes 2097152 | tf_op jit(solution)/shard_map/psum | solution.py:75
  9.6 16.3 %collective-permute-start.2 = (f32[2,1,1,120,512]{4,3,1,0,2:T(8,128)}, f32[2,1,1,120,512]{4,3,1,0,2:T(8,128)}, u32[]{:S(2)}, u32[]{:S(2)}) collective-permute-start(f32[2,1,1,120,512]{4,3,1,0,2:T(8,128)} %get-tuple-element.32), channel_id=1, source_target_pairs={{0,4},{4,8},{8,12},{12,0},{1,5},{5,9},{9,13},{13,1},{2,6},{6,10},{... | collective-permute-start | bytes 1474568 | tf_op jit(solution)/shard_map/ppermute | solution.py:16
  12.5 23.3 %collective-permute-start.3 = (f32[2,1,1,120,512]{4,3,1,0,2:T(8,128)}, f32[2,1,1,120,512]{4,3,1,0,2:T(8,128)}, u32[]{:S(2)}, u32[]{:S(2)}) collective-permute-start(f32[2,1,1,120,512]{4,3,1,0,2:T(8,128)} %get-tuple-element.33), channel_id=1, source_target_pairs={{4,0},{8,4},{12,8},{0,12},{5,1},{9,5},{13,9},{1,13},{6,2},{10,6},{... | collective-permute-start | bytes 1474568 | tf_op jit(solution)/shard_map/ppermute | solution.py:17
  13.6 2.2 copy-start.20
  13.6 2.8 copy-start.21
  13.6 4.4 %copy-start.12 = (f32[2,2,1,4,120]{4,3,2,1,0:T(4,128)S(1)}, f32[2,2,1,4,120]{4,3,2,1,0:T(4,128)}, u32[]{:S(2)}) copy-start(f32[2,2,1,4,120]{4,3,2,1,0:T(4,128)} %param.13) | copy-start | bytes 23044
  13.6 22.2 %copy-start.4 = (f32[2,3,1,120,512]{4,3,2,1,0:T(8,128)S(1)}, f32[2,3,1,120,512]{4,3,2,1,0:T(8,128)}, u32[]{:S(2)}) copy-start(f32[2,3,1,120,512]{4,3,2,1,0:T(8,128)} %param.12) | copy-start | bytes 4423684
  14.4 23.1 %collective-permute-start.1 = (f32[1,2,1,120,512]{4,3,0,1,2:T(8,128)}, f32[1,2,1,120,512]{4,3,0,1,2:T(8,128)}, u32[]{:S(2)}, u32[]{:S(2)}) collective-permute-start(f32[1,2,1,120,512]{4,3,0,1,2:T(8,128)} %copy.54), channel_id=1, source_target_pairs={{16,0},{0,16},{17,1},{1,17},{18,2},{2,18},{19,3},{3,19},{20,4},{4,... | collective-permute-start | bytes 1474568 | tf_op jit(solution)/shard_map/ppermute | solution.py:17
  15.3 22.3 %collective-permute-start = (f32[1,2,1,120,512]{4,3,0,1,2:T(8,128)}, f32[1,2,1,120,512]{4,3,0,1,2:T(8,128)}, u32[]{:S(2)}, u32[]{:S(2)}) collective-permute-start(f32[1,2,1,120,512]{4,3,0,1,2:T(8,128)} %copy.55), channel_id=1, source_target_pairs={{0,16},{16,0},{1,17},{17,1},{2,18},{18,2},{3,19},{19,3},{4,20},{20... | collective-permute-start | bytes 1474568 | tf_op jit(solution)/shard_map/ppermute | solution.py:16
  18.2 19.4 %copy-start.16 = (f32[3]{0:T(128)}, f32[3]{0:T(128)S(1)}, u32[]{:S(2)}) copy-start(f32[3]{0:T(128)S(1)} %pad.30.clone) | copy-start | bytes 40
  42.9 54.0 %copy-start.10 = (f32[1,1,128,512]{3,2,1,0:T(8,128)S(1)}, f32[1,1,128,512]{3,2,1,0:T(8,128)}, u32[]{:S(2)}) copy-start(f32[1,1,128,512]{3,2,1,0:T(8,128)} %param.20) | copy-start | bytes 786436
  44.6 106.7 %all-reduce.6.cloned.1.call-start = ((), (), s32[]{:S(2)}) async-start(), calls=%async_computation.1 | async-start | bytes 2097152 | tf_op jit(solution)/shard_map/psum | solution.py:83
  96.9 54.7 %copy-start.8 = (f32[512,512]{1,0:T(8,128)S(1)}, f32[512,512]{1,0:T(8,128)}, u32[]{:S(2)}) copy-start(f32[512,512]{1,0:T(8,128)} %all-reduce.4.cloned.1.call-done) | copy-start | bytes 3145732
  100.0 110.5 %all-reduce.8.cloned.1.call-start = ((), (), s32[]{:S(2)}) async-start(), calls=%async_computation.2 | async-start | bytes 2097152 | tf_op jit(solution)/shard_map/psum | solution.py:84
  151.3 93.7 %all-gather.2.cloned.1.call-start = ((), (), s32[]{:S(2)}) async-start(), calls=%async_computation.3 | async-start | bytes 1310720 | tf_op jit(solution)/shard_map/all_gather | solution.py:87
  155.0 58.9 %copy-start.11 = (f32[512,128]{1,0:T(8,128)S(1)}, f32[512,128]{1,0:T(8,128)}, u32[]{:S(2)}) copy-start(f32[512,128]{1,0:T(8,128)} %fusion.11) | copy-start | bytes 786436
  213.9 31.1 %copy-start.19 = (s32[256]{0:T(256)S(1)}, s32[256]{0:T(256)}, u32[]{:S(2)}) copy-start(s32[256]{0:T(256)} %eq.15) | copy-start | bytes 3076
  251.0 4.2 %collective-permute-start.5 = (f32[1,2,1,120,512]{4,3,0,1,2:T(8,128)S(1)}, f32[1,2,1,120,512]{4,3,0,1,2:T(8,128)S(1)}, u32[]{:S(2)}, u32[]{:S(2)}) collective-permute-start(f32[1,2,1,120,512]{4,3,0,1,2:T(8,128)S(1)} %get-tuple-element.17), channel_id=1, source_target_pairs={{16,0},{0,16},{17,1},{1,17},{18,2},{2,18},{19,3},{3,19},{20,4},{4,... | collective-permute-start | bytes 1474568 | tf_op jit(solution)/shard_map/ppermute | solution.py:17
  251.1 4.1 %collective-permute-start.4 = (f32[1,2,1,120,512]{4,3,0,1,2:T(8,128)S(1)}, f32[1,2,1,120,512]{4,3,0,1,2:T(8,128)S(1)}, u32[]{:S(2)}, u32[]{:S(2)}) collective-permute-start(f32[1,2,1,120,512]{4,3,0,1,2:T(8,128)S(1)} %get-tuple-element.18), channel_id=1, source_target_pairs={{0,16},{16,0},{1,17},{17,1},{2,18},{18,2},{3,19},{19,3},{4,20},{20... | collective-permute-start | bytes 1474568 | tf_op jit(solution)/shard_map/ppermute | solution.py:16
  252.2 3.1 %copy-start.17 = (f32[3]{0:T(128)S(1)}, f32[3]{0:T(128)}, u32[]{:S(2)}) copy-start(f32[3]{0:T(128)} %copy-done.16) | copy-start | bytes 40
  252.2 15.0 %collective-permute-start.6 = (f32[2,1,1,120,512]{4,3,0,2,1:T(8,128)S(1)}, f32[2,1,1,120,512]{4,3,0,2,1:T(8,128)S(1)}, u32[]{:S(2)}, u32[]{:S(2)}) collective-permute-start(f32[2,1,1,120,512]{4,3,0,2,1:T(8,128)S(1)} %get-tuple-element.24), channel_id=1, source_target_pairs={{0,4},{4,8},{8,12},{12,0},{1,5},{5,9},{9,13},{13,1},{2,6},{6,10},{... | collective-permute-start | bytes 1474568 | tf_op jit(solution)/shard_map/ppermute | solution.py:16
  252.7 23.2 %collective-permute-start.7 = (f32[2,1,1,120,512]{4,3,0,2,1:T(8,128)S(1)}, f32[2,1,1,120,512]{4,3,0,2,1:T(8,128)S(1)}, u32[]{:S(2)}, u32[]{:S(2)}) collective-permute-start(f32[2,1,1,120,512]{4,3,0,2,1:T(8,128)S(1)} %get-tuple-element.25), channel_id=1, source_target_pairs={{4,0},{8,4},{12,8},{0,12},{5,1},{9,5},{13,9},{1,13},{6,2},{10,6},{... | collective-permute-start | bytes 1474568 | tf_op jit(solution)/shard_map/ppermute | solution.py:17
  (10 other events, 17.0 us)
Sparse Core Ops, SparseCore 0:
  44.7 52.1 all-reduce.3
  100.1 51.1 all-reduce.5
  154.5 55.9 all-reduce.7
  215.8 29.2 all-gather.1
where the time goes:
time: 290 us
  waiting for transfers between devices  225 us (78%)
  matrix products  20.3 us (7%)
  between operations  14.2 us (5%)
  local copies, waits for them, and re-layouts  14 us (5%)
  starting transfers between devices  8.29 us (3%)
  other arithmetic  8.09 us (3%)
    psum x1, waiting for transfers between devices, on_device(): top_res = lax.psum(column_top, ('gx', 'gy'))  55.5 us
    psum x1, waiting for transfers between devices, on_device(): column_res = lax.psum(column_part, 'gz')  52.2 us
    psum x1, waiting for transfers between devices, on_device(): column_top = lax.psum(top_part, 'gz')  51.3 us
    all_gather x1, waiting for transfers between devices, on_device(): column_vals = lax.all_gather(value_rows, 'gz', axis=0, tiled=True)  29.3 us
    ppermute x4, waiting for transfers between devices, with_halo(): after = lax.ppermute(initial, axis, down)  18.6 us
    ppermute x4, waiting for transfers between devices, with_halo(): before = lax.ppermute(last, axis, up)  18 us
    unnamed x48, local copies, waits for them, and re-layouts  8.98 us
  transfers between devices with their start and end apart: 12, of which 8 were waited for; matrix products, arithmetic and copies ran while one was open for 4% of the time, Pallas kernels for 0%

commit v1 on v0

v1 whole, which is shorter than its diff:
```python
import functools

import jax
import jax.numpy as jnp
from jax import lax
from jax.experimental import pallas as pl
from jax.experimental.pallas import tpu as pltpu
from jax.sharding import PartitionSpec as P

BLK = 30
AXES = ("gx", "gy", "gz")
MESH = pl.DeviceIdType.MESH
F32 = jnp.float32
BF16 = jnp.bfloat16


def mm(a, b):
    return jnp.dot(a.astype(BF16), b.astype(BF16), preferred_element_type=F32)


def mm_t(a, b):
    return lax.dot_general(
        a.astype(BF16), b.astype(BF16), (((0,), (0,)), ((), ())), preferred_element_type=F32
    )


def kernel(
    sizes,
    owners,
    rx,
    ry,
    scale,
    live,
    neumann,
    schur,
    basis,
    cmap,
    inv,
    cbas,
    top,
    zx,
    zy,
    image,
    hx1,
    hy1,
    hx2,
    hy2,
    ubuf,
    wbuf,
    graw,
    raw,
    maps,
    minv,
    mbas,
    g3p,
    rs,
    part,
    g3,
    vout,
    vall,
    h1_s,
    h1_r,
    h2_s,
    h2_r,
    mat_s,
    mat_r,
    raw_s,
    raw_r,
    rs_s,
    rs_r,
    ag_s,
    ag_r,
    v_s,
    v_r,
):
    gx_n, gy_n, gz_n = sizes
    x, y, z = (lax.axis_index(a) for a in AXES)
    layer_n = gx_n * gy_n
    mine = x * gy_n + y
    halves = len(owners)
    width = rx.shape[3] // halves
    ni, nj = rx.shape[0] - 1, ry.shape[1] - 1
    coarse = basis.shape[2]
    rows = inv.shape[0]
    slab = part.shape[0]

    def cols(h):
        return slice(h * width, (h + 1) * width)

    def copy(src, dst, send, recv, to):
        return pltpu.make_async_remote_copy(
            src_ref=src, dst_ref=dst, send_sem=send, recv_sem=recv, device_id=to, device_id_type=MESH
        )

    def layer_peer(d):
        p = lax.rem(mine + d, layer_n)
        return (p // gy_n, lax.rem(p, gy_n), z)

    barrier = pltpu.get_barrier_semaphore()
    for d in range(1, layer_n):
        pl.semaphore_signal(barrier, inc=1, device_id=layer_peer(d), device_id_type=MESH)
    for d in range(1, gz_n):
        pl.semaphore_signal(
            barrier, inc=1, device_id=(x, y, lax.rem(z + d, gz_n)), device_id_type=MESH
        )
    pl.semaphore_wait(barrier, layer_n - 1 + gz_n - 1)

    x_up, x_down = (lax.rem(x + 1, gx_n), y, z), (lax.rem(x + gx_n - 1, gx_n), y, z)
    y_up, y_down = (x, lax.rem(y + 1, gy_n), z), (x, lax.rem(y + gy_n - 1, gy_n), z)

    def halo(fx, fy, hx, hy, send, recv, h):
        c = cols(h)
        s, r = send.at[h], recv.at[h]
        return [
            copy(fy.at[:, nj, :, c], hy.at[0, :, :, c], s.at[0], r.at[0], y_up),
            copy(fy.at[:, 0, :, c], hy.at[1, :, :, c], s.at[1], r.at[1], y_down),
            copy(fx.at[ni, :, :, c], hx.at[0, :, :, c], s.at[2], r.at[2], x_up),
            copy(fx.at[0, :, :, c], hx.at[1, :, :, c], s.at[3], r.at[3], x_down),
        ]

    own_rows = pl.ds(pl.multiple_of(z * rows, rows), rows)

    def matrices(k):
        to = (x, y, owners[k])
        return [
            copy(inv, minv.at[own_rows], mat_s.at[k, 0], mat_r.at[0, z], to),
            copy(cbas, mbas.at[own_rows], mat_s.at[k, 1], mat_r.at[1, z], to),
            copy(cmap, maps.at[z], mat_s.at[k, 2], mat_r.at[2, z], to),
        ]

    first = [halo(rx, ry, hx1, hy1, h1_s, h1_r, h) for h in range(halves)]
    for c in first[0]:
        c.start()
    for k in range(halves):

        @pl.when(z != owners[k])
        def _():
            for c in matrices(k):
                c.start()

        @pl.when(z == owners[k])
        def _():
            minv[own_rows] = inv[...]
            mbas[own_rows] = cbas[...]
            maps[z] = cmap[...]

    for h in range(1, halves):
        for c in first[h]:
            c.start()

    def stack_faces(xf, yf, i, j):
        return jnp.concatenate([xf(i, j), xf(i + 1, j), yf(i, j), yf(i, j + 1)], 0)

    for h in range(halves):
        c = cols(h)
        for f in first[h]:
            f.wait_recv()

        def xf(q, j):
            own = rx[q, j, :, c]
            return own if 0 < q < ni else own + hx1[0 if q == 0 else 1, j, :, c]

        def yf(i, q):
            own = ry[i, q, :, c]
            return own if 0 < q < nj else own + hy1[0 if q == 0 else 1, i, :, c]

        for i in range(ni):
            for j in range(nj):
                s = i * nj + j
                u = (stack_faces(xf, yf, i, j) * scale[s]).astype(BF16)
                ubuf[s, :, c] = u
                graw[h, s * coarse : (s + 1) * coarse] = mm_t(basis[s], u)
        o = owners[h]

        @pl.when(z != o)
        def _():
            copy(graw.at[h], raw.at[z], raw_s.at[h], raw_r.at[z], (x, y, o)).start()

        @pl.when(z == o)
        def _():
            raw[z] = graw[h]

    for s in range(ni * nj):
        wbuf[s] = jnp.dot(neumann[s], ubuf[s], preferred_element_type=F32)

    def select(zz):
        picks = lax.broadcasted_iota(jnp.int32, (minv.shape[0], cmap.shape[1]), 0)
        return (picks == maps[zz, 0:1]).astype(F32).astype(BF16)

    which = z - owners[0]

    def back(zz):
        return copy(vout.at[zz], vall.at[which], v_s.at[zz], v_r.at[which], (x, y, zz))

    @pl.when((z >= owners[0]) & (z <= owners[-1]))
    def _():
        for zz in range(gz_n):

            @pl.when(z != zz)
            def _():
                copy(graw.at[0], raw.at[zz], raw_s.at[0], raw_r.at[zz], (x, y, zz)).wait_recv()
                there = pl.ds(zz * rows, rows)
                copy(cmap, maps.at[zz], mat_s.at[0, 2], mat_r.at[2, zz], (x, y, zz)).wait_recv()
                copy(inv, minv.at[there], mat_s.at[0, 0], mat_r.at[0, zz], (x, y, zz)).wait_recv()
                copy(cbas, mbas.at[there], mat_s.at[0, 1], mat_r.at[1, zz], (x, y, zz)).wait_recv()

        g2 = lax.fori_loop(
            0,
            gz_n,
            lambda zz, acc: acc + mm(select(zz), raw[zz]),
            jnp.zeros((minv.shape[0], width), F32),
        ).astype(BF16)
        g3p[...] = mm_t(mbas[...], g2)

        def scatter(d):
            to = layer_peer(d)
            there = pl.ds(pl.multiple_of((to[0] * gy_n + to[1]) * slab, slab), slab)
            return copy(g3p.at[there], rs.at[d - 1], rs_s.at[d - 1], rs_r.at[d - 1], to)

        own_slab = pl.ds(pl.multiple_of(mine * slab, slab), slab)

        def gather(d):
            return copy(part, g3.at[own_slab], ag_s.at[d - 1], ag_r.at[d - 1], layer_peer(d))

        def gathered(d):
            q = lax.rem(mine + layer_n - d, layer_n)
            there = pl.ds(pl.multiple_of(q * slab, slab), slab)
            return copy(part, g3.at[there], ag_s.at[d - 1], ag_r.at[d - 1], layer_peer(d))

        for d in range(1, layer_n):
            scatter(d).start()
        y2 = mm(minv[...], g2)
        total = g3p[own_slab]
        for d in range(1, layer_n):
            scatter(d).wait_recv()
            total = total + rs[d - 1]
        part[...] = total
        g3[own_slab] = total
        for d in range(1, layer_n):
            gather(d).start()
        for d in range(1, layer_n):
            gathered(d).wait_recv()
        y3 = mm(top[...], g3[...])
        v2 = (y2 + mm(mbas[...], y3)).astype(BF16)
        for zz in range(gz_n):
            vout[zz] = mm_t(select(zz), v2)

            @pl.when(z != zz)
            def _():
                back(zz).start()

            @pl.when(z == zz)
            def _():
                vall[which] = vout[zz]

        for d in range(1, layer_n):
            scatter(d).wait_send()
            gather(d).wait_send()

    second = [halo(zx, zy, hx2, hy2, h2_s, h2_r, h) for h in range(halves)]
    for h in range(halves):
        c = cols(h)
        o = owners[h]

        @pl.when(z != o)
        def _():
            copy(vout.at[0], vall.at[h], v_s.at[0], v_r.at[h], (x, y, o)).wait_recv()

        face = rx.shape[2]
        for i in range(ni):
            for j in range(nj):
                s = i * nj + j
                v = vall[h, s * coarse : (s + 1) * coarse].astype(BF16)
                con = (
                    wbuf[s, :, c] + jnp.dot(basis[s], v, preferred_element_type=F32)
                ) * scale[s]
                c0, c1, c2, c3 = (con[k * face : (k + 1) * face] for k in range(4))
                zx[i, j, :, c] = c0 if i == 0 else zx[i, j, :, c] + c0
                zx[i + 1, j, :, c] = c1
                zy[i, j, :, c] = c2 if j == 0 else zy[i, j, :, c] + c2
                zy[i, j + 1, :, c] = c3
        for f in second[h]:
            f.start()

    for h in range(halves):
        c = cols(h)
        for f in second[h]:
            f.wait()
        for j in range(nj):
            zx[0, j, :, c] += hx2[0, j, :, c]
            zx[ni, j, :, c] += hx2[1, j, :, c]
        for i in range(ni):
            zy[i, 0, :, c] += hy2[0, i, :, c]
            zy[i, nj, :, c] += hy2[1, i, :, c]
        for i in range(ni):
            for j in range(nj):
                s = i * nj + j
                zs = stack_faces(
                    lambda q, jj: zx[q, jj, :, c], lambda ii, q: zy[ii, q, :, c], i, j
                )
                zs = (zs * live[s]).astype(BF16)
                image[s, :, c] = jnp.dot(schur[s], zs, preferred_element_type=F32).astype(BF16)

    for h in range(halves):
        for f in first[h]:
            f.wait_send()
        o = owners[h]

        @pl.when(z != o)
        def _():
            for f in matrices(h):
                f.wait_send()
            copy(graw.at[h], raw.at[z], raw_s.at[h], raw_r.at[z], (x, y, o)).wait_send()

    @pl.when((z >= owners[0]) & (z <= owners[-1]))
    def _():
        for zz in range(gz_n):

            @pl.when(z != zz)
            def _():
                back(zz).wait_send()


def on_device(
    sizes,
    resid_x,
    resid_y,
    face_weights,
    face_counts,
    neumann,
    schur,
    basis,
    coarse_map,
    column_inverse,
    column_basis,
    top_inverse,
):
    gx_n, gy_n, gz_n = sizes
    layer_n = gx_n * gy_n
    owners = ((gz_n - 1) // 2, gz_n // 2) if gz_n % 2 == 0 else (gz_n // 2,)
    halves = len(owners)
    face, loads = resid_x.shape[3:]
    inner = neumann.shape[3]
    coarse = basis.shape[4]
    subs = neumann.shape[0] * neumann.shape[1]
    rx = resid_x[:, :, 0]
    ry = resid_y[:, :, 0]
    dof = jnp.arange(face, dtype=jnp.int32)
    live = (dof < face_counts[:, :, 0, :, None] * BLK).astype(F32)
    scale = (face_weights[:, :, 0] * live).reshape(subs, inner, 1)
    live = live.reshape(subs, inner, 1)
    local = subs * coarse
    cmap = jnp.broadcast_to(coarse_map.reshape(1, local), (8, local))
    inv, cbas = column_inverse[0, 0], column_basis[0, 0]
    nc2, nc3 = inv.shape[1], top_inverse.shape[0]
    width = loads // halves
    slab = nc3 // layer_n
    dma = pltpu.SemaphoreType.DMA
    vm = pltpu.VMEM
    nx, ny = rx.shape[1], ry.shape[0]
    spec = pl.BlockSpec(memory_space=pltpu.VMEM)
    z_x, z_y, image = pl.pallas_call(
        functools.partial(kernel, sizes, owners),
        out_shape=(
            jax.ShapeDtypeStruct(rx.shape, F32),
            jax.ShapeDtypeStruct(ry.shape, F32),
            jax.ShapeDtypeStruct((subs, inner, loads), BF16),
        ),
        in_specs=[spec] * 11,
        out_specs=(spec,) * 3,
        scratch_shapes=[
            vm((2, nx, face, loads), F32),
            vm((2, ny, face, loads), F32),
            vm((2, nx, face, loads), F32),
            vm((2, ny, face, loads), F32),
            vm((subs, inner, loads), BF16),
            vm((subs, inner, loads), F32),
            vm((halves, local, width), F32),
            vm((gz_n, local, width), F32),
            vm((gz_n, 8, local), jnp.int32),
            vm((nc2, nc2), F32),
            vm((nc2, nc3), F32),
            vm((nc3, width), F32),
            vm((layer_n - 1, slab, width), F32),
            vm((slab, width), F32),
            vm((nc3, width), F32),
            vm((gz_n, local, width), F32),
            vm((halves, local, width), F32),
            dma((halves, 4)),
            dma((halves, 4)),
            dma((halves, 4)),
            dma((halves, 4)),
            dma((halves, 3)),
            dma((3, gz_n)),
            dma((halves,)),
            dma((gz_n,)),
            dma((layer_n - 1,)),
            dma((layer_n - 1,)),
            dma((layer_n - 1,)),
            dma((layer_n - 1,)),
            dma((gz_n,)),
            dma((halves,)),
        ],
        compiler_params=pltpu.CompilerParams(
            collective_id=0, has_side_effects=True, vmem_limit_bytes=56 * 1024 * 1024
        ),
        name="bddc",
    )(
        rx,
        ry,
        scale,
        live,
        neumann.reshape(subs, inner, inner),
        schur.reshape(subs, inner, inner),
        basis.reshape(subs, inner, coarse),
        cmap,
        inv,
        cbas,
        top_inverse,
    )
    return (
        z_x[:, :, None],
        z_y[:, :, None],
        image.reshape(neumann.shape[0], neumann.shape[1], 1, inner, loads),
    )


def solution(mesh):
    sizes = tuple(mesh.shape[a] for a in AXES)
    vec, mat = P("gx", "gy", "gz", None), P("gx", "gy", "gz", None, None)
    return jax.shard_map(
        functools.partial(on_device, sizes),
        mesh=mesh,
        in_specs=(mat, mat, mat, vec, mat, mat, mat, vec, vec, vec, P()),
        out_specs=(mat, mat, mat),
        check_vma=False,
    )
```

time: 290 us -> 117 us (0.40)
  waiting for transfers between devices: 225 us -> 0 us
  Pallas kernels: 0 us -> 102 us
  matrix products: 20.3 us -> 0 us
  between operations: 14.2 us -> 0.67 us
  starting transfers between devices: 8.29 us -> 0 us
  local copies, waits for them, and re-layouts: 14 us -> 10.1 us
  other arithmetic: 8.09 us -> 4.25 us
    psum x3 -> x0, waiting for transfers between devices: 159 us -> none  [the longest x1 55.5 us: on_device(): top_res = lax.psum(column_top, ('gx', 'gy'))]
    pallas_call x0 -> x1, Pallas kernels: none -> 102 us  [on_device(): pl.pallas_call(functools.partial(kernel, sizes, owners), out_shape=(jax.S...]
    ppermute x8 -> x0, waiting for transfers between devices: 36.6 us -> none  [the longest x4 18.6 us: with_halo(): after = lax.ppermute(initial, axis, down)]
    all_gather x1 -> x0, waiting for transfers between devices: 29.3 us -> none  [on_device(): column_vals = lax.all_gather(value_rows, 'gz', axis=0, tiled=True)]
    dot_general x10 -> x0, matrix products: 20.3 us -> none  [the longest x1 3.46 us: on_device(): level_two = jnp.dot(inverse_rows, column_res, precision=high)]
    ppermute x8 -> x0, starting transfers between devices: 7.95 us -> none  [the longest x4 4.45 us: with_halo(): before = lax.ppermute(last, axis, up)]
    unnamed x48 -> x11, local copies, waits for them, and re-layouts: 8.98 us -> 8.6 us
  transfers between devices with their start and end apart: 12 -> 0, of which waited for: 8 -> 0; matrix products, arithmetic and copies ran while one was open for 4% -> 0% of each run, Pallas kernels for 0% -> 0%
where the time goes in v1:
time: 117 us
  Pallas kernels  102 us (87%)
  local copies, waits for them, and re-layouts  10.1 us (9%)
  other arithmetic  4.25 us (4%)
    pallas_call x1, Pallas kernels, on_device(): pl.pallas_call(functools.partial(kernel, sizes, owners), out_shape=(jax.S...  102 us
    unnamed x11, local copies, waits for them, and re-layouts  8.6 us

profile of v1, /device:TPU:0, one launch (start us, length us, event | category | flops | bytes accessed | tf_op | source)
XLA Modules:
  0.0 117.2 jit_solution(1485767780555171529)
XLA Ops:
  0.6 0.5 broadcast.56
  1.1 1.3 %reduce.3 = s32[2,2,64]{2,1,0:T(2,128)S(1)} reduce(s32[2,2,1,64]{3,2,1,0:T(1,128)} %param.18, s32[]{:T(128)} %broadcast.56), dimensions={2}, to_apply=%param.18.reduce_sub_computation.3 | reduce | bytes 2052 | tf_op args[7]
  2.5 0.1 broadcast_in_dim.14
  2.6 0.7 broadcast_multiply_fusion
  3.3 0.1 lt.31
  3.3 0.1 lt.33
  3.4 0.6 broadcast_in_dim.15.cmap
  4.0 1.9 %copy.20 = bf16[2,2,1,480,64]{4,3,1,0,2:T(8,128)(2,1)} copy(bf16[2,2,1,480,64]{3,4,2,1,0:T(8,128)(2,1)} %param.17) | data formatting | bytes 491520 | tf_op args[6]
  6.0 0.0 copy-start.2
  6.0 0.3 lt.36
  6.3 1.2 %fusion = (f32[4,480,1]{2,1,0:T(8,128)}, pred[4,480,1]{2,1,0:T(8,128)(4,1)S(1)}) fusion(s32[4,480,1]{2,1,0:T(8,128)S(1)} %lt.36, s32[480]{0:T(512)S(1)} %lt.31), kind=kLoop, calls=%fused_computation.3 | loop fusion | flops 3840 | bytes 19200 | tf_op jit(solution)/shard_map/convert_element_type | solution.py:349
  7.5 0.0 copy-done.2
  7.5 0.3 squeeze.20
  7.8 1.0 broadcast_select_fusion.scale
  8.9 102.2 %bddc.1 = (f32[3,2,120,512]{3,2,1,0:T(8,128)}, f32[2,3,120,512]{3,2,1,0:T(8,128)}, bf16[4,480,512]{2,1,0:T(8,128)(2,1)}) custom-call(f32[3,2,120,512]{3,2,1,0:T(8,128)} %bitcast.21, f32[2,3,120,512]{3,2,1,0:T(8,128)} %bitcast.22, f32[4,480,1]{2,1,0:T(8,128)} %broadcast_select_fusion.scale, f32[4,480,1]{2,1,0:T(8,128)} %get-tuple-element.15.live, ...), custom_call_target="tpu_custom_call" | custom-call | tf_op jit(solution)/shard_map/bddc/pallas_call | solution.py:362
  111.1 0.0 copy-start.1
  111.1 2.8 %copy.27 = f32[3,2,1,120,512]{4,3,2,1,0:T(8,128)} copy(f32[3,2,1,120,512]{4,3,2,1,0:T(8,128)} %bitcast.24) | data formatting | bytes 2949120
  113.9 0.0 copy-done.1
  113.9 0.0 copy-start
  113.9 1.1 copy.28
  115.0 1.0 copy-done
  115.9 1.3 %copy.29 = bf16[2,2,1,480,512]{4,3,2,1,0:T(8,128)(2,1)} copy(bf16[2,2,1,480,512]{4,3,2,1,0:T(8,128)(2,1)S(1)} %bitcast.19) | data formatting | bytes 3932160
  (1 shorter events, 0.0 us)
Async XLA Ops:
  6.0 1.5 %copy-start.2 = (f32[2,2,1,4,120]{4,3,2,1,0:T(4,128)S(1)}, f32[2,2,1,4,120]{4,3,2,1,0:T(4,128)}, u32[]{:S(2)}) copy-start(f32[2,2,1,4,120]{4,3,2,1,0:T(4,128)} %param.13) | copy-start | bytes 23044
  111.1 2.8 %copy-start.1 = (f32[2,3,120,512]{3,2,1,0:T(8,128)S(1)}, f32[2,3,120,512]{3,2,1,0:T(8,128)}, u32[]{:S(2)}) copy-start(f32[2,3,120,512]{3,2,1,0:T(8,128)} %get-tuple-element.7) | copy-start | bytes 4423684
  113.9 2.1 %copy-start = (bf16[4,480,512]{2,1,0:T(8,128)(2,1)S(1)}, bf16[4,480,512]{2,1,0:T(8,128)(2,1)}, u32[]{:S(2)}) copy-start(bf16[4,480,512]{2,1,0:T(8,128)(2,1)} %get-tuple-element.8) | copy-start | bytes 5898244

commit v2 on v1

--- a/solution.py
+++ b/solution.py
@@ -18,6 +18,19 @@
     return jnp.dot(a.astype(BF16), b.astype(BF16), preferred_element_type=F32)
 
 
+def live_mask(counts, i, j, face):
+    index = lax.broadcasted_iota(jnp.int32, (face, counts.shape[2]), 0)
+    return (index < counts[i, j : j + 1] * BLK).astype(F32)
+
+
+def column(faces):
+    return jnp.concatenate([faces[:, k : k + 1] for k in range(faces.shape[1])], 0)
+
+
+def stack_faces(xf, yf, i, j):
+    return jnp.concatenate([xf(i, j), xf(i + 1, j), yf(i, j), yf(i, j + 1)], 0)
+
+
 def mm_t(a, b):
     return lax.dot_general(
         a.astype(BF16), b.astype(BF16), (((0,), (0,)), ((), ())), preferred_element_type=F32
@@ -27,20 +40,24 @@
 def kernel(
     sizes,
     owners,
+    rx_hbm,
+    ry_hbm,
+    weights,
+    counts,
+    neumann_hbm,
+    basis,
+    targets,
+    inv,
+    cbas,
+    top_hbm,
+    zx,
+    zy,
     rx,
     ry,
+    neumann,
+    top,
     scale,
-    live,
-    neumann,
-    schur,
-    basis,
     cmap,
-    inv,
-    cbas,
-    top,
-    zx,
-    zy,
-    image,
     hx1,
     hy1,
     hx2,
@@ -53,7 +70,9 @@
     minv,
     mbas,
     g3p,
-    rs,
+    rs1,
+    sum1,
+    rs2,
     part,
     g3,
     vout,
@@ -66,12 +85,17 @@
     mat_r,
     raw_s,
     raw_r,
-    rs_s,
-    rs_r,
-    ag_s,
-    ag_r,
+    rs1_s,
+    rs1_r,
+    rs2_s,
+    rs2_r,
+    ag1_s,
+    ag1_r,
+    ag2_s,
+    ag2_r,
     v_s,
     v_r,
+    in_s,
 ):
     gx_n, gy_n, gz_n = sizes
     x, y, z = (lax.axis_index(a) for a in AXES)
@@ -85,7 +109,7 @@
     slab = part.shape[0]
 
     def cols(h):
-        return slice(h * width, (h + 1) * width)
+        return pl.ds(pl.multiple_of(h * width, width), width)
 
     def copy(src, dst, send, recv, to):
         return pltpu.make_async_remote_copy(
@@ -95,6 +119,17 @@
     def layer_peer(d):
         p = lax.rem(mine + d, layer_n)
         return (p // gy_n, lax.rem(p, gy_n), z)
+
+    loads_in = [
+        pltpu.make_async_copy(a, b, in_s.at[k])
+        for k, (a, b) in enumerate(
+            ((rx_hbm, rx), (ry_hbm, ry), (neumann_hbm, neumann), (top_hbm, top))
+        )
+    ]
+    for c in loads_in:
+        c.start()
+    lists = [targets[i, j : j + 1] for i in range(ni) for j in range(nj)]
+    cmap[...] = jnp.broadcast_to(jnp.concatenate(lists, 1), cmap.shape)
 
     barrier = pltpu.get_barrier_semaphore()
     for d in range(1, layer_n):
@@ -128,7 +163,7 @@
             copy(cmap, maps.at[z], mat_s.at[k, 2], mat_r.at[2, z], to),
         ]
 
-    first = [halo(rx, ry, hx1, hy1, h1_s, h1_r, h) for h in range(halves)]
+    first = [halo(rx_hbm, ry_hbm, hx1, hy1, h1_s, h1_r, h) for h in range(halves)]
     for c in first[0]:
         c.start()
     for k in range(halves):
@@ -148,8 +183,11 @@
         for c in first[h]:
             c.start()
 
-    def stack_faces(xf, yf, i, j):
-        return jnp.concatenate([xf(i, j), xf(i + 1, j), yf(i, j), yf(i, j + 1)], 0)
+    for i in range(ni):
+        for j in range(nj):
+            scale[i * nj + j] = column(weights[i, j].T * live_mask(counts, i, j, rx.shape[2]))
+    loads_in[0].wait()
+    loads_in[1].wait()
 
     for h in range(halves):
         c = cols(h)
@@ -180,6 +218,7 @@
         def _():
             raw[z] = graw[h]
 
+    loads_in[2].wait()
     for s in range(ni * nj):
         wbuf[s] = jnp.dot(neumann[s], ubuf[s], preferred_element_type=F32)
 
@@ -187,12 +226,19 @@
         picks = lax.broadcasted_iota(jnp.int32, (minv.shape[0], cmap.shape[1]), 0)
         return (picks == maps[zz, 0:1]).astype(F32).astype(BF16)
 
+    loads_in[3].wait()
     which = z - owners[0]
+    is_owner = (z >= owners[0]) & (z <= owners[-1])
+
+    def far(zz):
+        if zz < owners[0]:
+            return z > owners[0]
+        return z < owners[-1] if zz > owners[-1] else z < 0
 
     def back(zz):
         return copy(vout.at[zz], vall.at[which], v_s.at[zz], v_r.at[which], (x, y, zz))
 
-    @pl.when((z >= owners[0]) & (z <= owners[-1]))
+    @pl.when(is_owner)
     def _():
         for zz in range(gz_n):
 
@@ -212,40 +258,65 @@
         ).astype(BF16)
         g3p[...] = mm_t(mbas[...], g2)
 
-        def scatter(d):
-            to = layer_peer(d)
-            there = pl.ds(pl.multiple_of((to[0] * gy_n + to[1]) * slab, slab), slab)
-            return copy(g3p.at[there], rs.at[d - 1], rs_s.at[d - 1], rs_r.at[d - 1], to)
-
+        def x_peer(d):
+            return (lax.rem(x + d, gx_n), y, z)
+
+        def y_peer(d):
+            return (x, lax.rem(y + d, gy_n), z)
+
+        half = slab * gy_n
+        own_half = pl.ds(pl.multiple_of(x * half, half), half)
+        own_part = pl.ds(pl.multiple_of(y * slab, slab), slab)
         own_slab = pl.ds(pl.multiple_of(mine * slab, slab), slab)
 
-        def gather(d):
-            return copy(part, g3.at[own_slab], ag_s.at[d - 1], ag_r.at[d - 1], layer_peer(d))
-
-        def gathered(d):
-            q = lax.rem(mine + layer_n - d, layer_n)
-            there = pl.ds(pl.multiple_of(q * slab, slab), slab)
-            return copy(part, g3.at[there], ag_s.at[d - 1], ag_r.at[d - 1], layer_peer(d))
-
-        for d in range(1, layer_n):
-            scatter(d).start()
+        def scatter_x(d):
+            to = x_peer(d)
+            there = pl.ds(pl.multiple_of(to[0] * half, half), half)
+            return copy(g3p.at[there], rs1.at[d - 1], rs1_s.at[d - 1], rs1_r.at[d - 1], to)
+
+        def scatter_y(d):
+            to = y_peer(d)
+            there = pl.ds(pl.multiple_of(to[1] * slab, slab), slab)
+            return copy(sum1.at[there], rs2.at[d - 1], rs2_s.at[d - 1], rs2_r.at[d - 1], to)
+
+        def gather_y(d, source):
+            rows_y = pl.ds(pl.multiple_of((x * gy_n + source) * slab, slab), slab)
+            return copy(part, g3.at[rows_y], ag1_s.at[d - 1], ag1_r.at[d - 1], y_peer(d))
+
+        def gather_x(d, source):
+            rows_x = pl.ds(pl.multiple_of(source * half, half), half)
+            return copy(g3.at[own_half], g3.at[rows_x], ag2_s.at[d - 1], ag2_r.at[d - 1], x_peer(d))
+
+        for d in range(1, gx_n):
+            scatter_x(d).start()
         y2 = mm(minv[...], g2)
-        total = g3p[own_slab]
-        for d in range(1, layer_n):
-            scatter(d).wait_recv()
-            total = total + rs[d - 1]
+        total = g3p[own_half]
+        for d in range(1, gx_n):
+            scatter_x(d).wait_recv()
+            total = total + rs1[d - 1]
+        sum1[...] = total
+        for d in range(1, gy_n):
+            scatter_y(d).start()
+        total = sum1[own_part]
+        for d in range(1, gy_n):
+            scatter_y(d).wait_recv()
+            total = total + rs2[d - 1]
         part[...] = total
         g3[own_slab] = total
-        for d in range(1, layer_n):
-            gather(d).start()
-        for d in range(1, layer_n):
-            gathered(d).wait_recv()
+        for d in range(1, gy_n):
+            gather_y(d, y).start()
+        for d in range(1, gy_n):
+            gather_y(d, lax.rem(y + gy_n - d, gy_n)).wait_recv()
+        for d in range(1, gx_n):
+            gather_x(d, x).start()
+        for d in range(1, gx_n):
+            gather_x(d, lax.rem(x + gx_n - d, gx_n)).wait_recv()
         y3 = mm(top[...], g3[...])
         v2 = (y2 + mm(mbas[...], y3)).astype(BF16)
         for zz in range(gz_n):
             vout[zz] = mm_t(select(zz), v2)
 
-            @pl.when(z != zz)
+            @pl.when((z != zz) & jnp.logical_not(far(zz)))
             def _():
                 back(zz).start()
 
@@ -253,20 +324,25 @@
             def _():
                 vall[which] = vout[zz]
 
-        for d in range(1, layer_n):
-            scatter(d).wait_send()
-            gather(d).wait_send()
-
-    second = [halo(zx, zy, hx2, hy2, h2_s, h2_r, h) for h in range(halves)]
-    for h in range(halves):
+        for d in range(1, gx_n):
+            scatter_x(d).wait_send()
+            gather_x(d, x).wait_send()
+        for d in range(1, gy_n):
+            scatter_y(d).wait_send()
+            gather_y(d, y).wait_send()
+
+    turn = z // ((gz_n + 1) // 2) if halves > 1 else 0
+    order = [lax.rem(k + turn, halves) for k in range(halves)]
+    second = [halo(zx, zy, hx2, hy2, h2_s, h2_r, h) for h in order]
+    face = rx.shape[2]
+    for k, h in enumerate(order):
         c = cols(h)
-        o = owners[h]
+        o = owners[0] + h
 
         @pl.when(z != o)
         def _():
             copy(vout.at[0], vall.at[h], v_s.at[0], v_r.at[h], (x, y, o)).wait_recv()
 
-        face = rx.shape[2]
         for i in range(ni):
             for j in range(nj):
                 s = i * nj + j
@@ -279,12 +355,27 @@
                 zx[i + 1, j, :, c] = c1
                 zy[i, j, :, c] = c2 if j == 0 else zy[i, j, :, c] + c2
                 zy[i, j + 1, :, c] = c3
-        for f in second[h]:
+        for f in second[k]:
             f.start()
-
-    for h in range(halves):
+        if k == 0:
+
+            @pl.when(is_owner)
+            def _():
+                for zz in range(gz_n):
+
+                    @pl.when((z != zz) & jnp.logical_not(far(zz)))
+                    def _():
+                        back(zz).wait_send()
+
+                for zz in range(gz_n):
+
+                    @pl.when(far(zz))
+                    def _():
+                        back(zz).start()
+
+    for k, h in enumerate(order):
         c = cols(h)
-        for f in second[h]:
+        for f in second[k]:
             f.wait()
         for j in range(nj):
             zx[0, j, :, c] += hx2[0, j, :, c]
@@ -292,14 +383,6 @@
         for i in range(ni):
             zy[i, 0, :, c] += hy2[0, i, :, c]
             zy[i, nj, :, c] += hy2[1, i, :, c]
-        for i in range(ni):
-            for j in range(nj):
-                s = i * nj + j
-                zs = stack_faces(
-                    lambda q, jj: zx[q, jj, :, c], lambda ii, q: zy[ii, q, :, c], i, j
-                )
-                zs = (zs * live[s]).astype(BF16)
-                image[s, :, c] = jnp.dot(schur[s], zs, preferred_element_type=F32).astype(BF16)
 
     for h in range(halves):
         for f in first[h]:
@@ -312,13 +395,25 @@
                 f.wait_send()
             copy(graw.at[h], raw.at[z], raw_s.at[h], raw_r.at[z], (x, y, o)).wait_send()
 
-    @pl.when((z >= owners[0]) & (z <= owners[-1]))
+    @pl.when(is_owner)
     def _():
         for zz in range(gz_n):
 
-            @pl.when(z != zz)
+            @pl.when(far(zz))
             def _():
                 back(zz).wait_send()
+
+
+def image_kernel(zx, zy, counts, schur, out_x, out_y, image):
+    out_x[...] = zx[...]
+    out_y[...] = zy[...]
+    ni, nj = zx.shape[0] - 1, zy.shape[1] - 1
+    for i in range(ni):
+        for j in range(nj):
+            s = i * nj + j
+            zs = stack_faces(lambda q, jj: zx[q, jj], lambda ii, q: zy[ii, q], i, j)
+            zs = (zs * column(live_mask(counts, i, j, zx.shape[2]))).astype(BF16)
+            image[s] = jnp.dot(schur[s], zs, preferred_element_type=F32).astype(BF16)
 
 
 def on_device(
@@ -345,12 +440,9 @@
     subs = neumann.shape[0] * neumann.shape[1]
     rx = resid_x[:, :, 0]
     ry = resid_y[:, :, 0]
-    dof = jnp.arange(face, dtype=jnp.int32)
-    live = (dof < face_counts[:, :, 0, :, None] * BLK).astype(F32)
-    scale = (face_weights[:, :, 0] * live).reshape(subs, inner, 1)
-    live = live.reshape(subs, inner, 1)
+    weights = face_weights[:, :, 0]
+    counts = face_counts[:, :, 0]
     local = subs * coarse
-    cmap = jnp.broadcast_to(coarse_map.reshape(1, local), (8, local))
     inv, cbas = column_inverse[0, 0], column_basis[0, 0]
     nc2, nc3 = inv.shape[1], top_inverse.shape[0]
     width = loads // halves
@@ -359,16 +451,22 @@
     vm = pltpu.VMEM
     nx, ny = rx.shape[1], ry.shape[0]
     spec = pl.BlockSpec(memory_space=pltpu.VMEM)
-    z_x, z_y, image = pl.pallas_call(
+    hbm = pl.BlockSpec(memory_space=pl.ANY)
+    zx, zy = pl.pallas_call(
         functools.partial(kernel, sizes, owners),
         out_shape=(
             jax.ShapeDtypeStruct(rx.shape, F32),
             jax.ShapeDtypeStruct(ry.shape, F32),
-            jax.ShapeDtypeStruct((subs, inner, loads), BF16),
         ),
-        in_specs=[spec] * 11,
-        out_specs=(spec,) * 3,
+        in_specs=[hbm, hbm, spec, spec, hbm, spec, spec, spec, spec, hbm],
+        out_specs=(spec, spec),
         scratch_shapes=[
+            vm(rx.shape, F32),
+            vm(ry.shape, F32),
+            vm((subs, inner, inner), BF16),
+            vm(top_inverse.shape, F32),
+            vm((subs, inner, 1), F32),
+            vm((8, local), jnp.int32),
             vm((2, nx, face, loads), F32),
             vm((2, ny, face, loads), F32),
             vm((2, nx, face, loads), F32),
@@ -381,7 +479,9 @@
             vm((nc2, nc2), F32),
             vm((nc2, nc3), F32),
             vm((nc3, width), F32),
-            vm((layer_n - 1, slab, width), F32),
+            vm((gx_n - 1, nc3 // gx_n, width), F32),
+            vm((nc3 // gx_n, width), F32),
+            vm((gy_n - 1, slab, width), F32),
             vm((slab, width), F32),
             vm((nc3, width), F32),
             vm((gz_n, local, width), F32),
@@ -394,12 +494,17 @@
             dma((3, gz_n)),
             dma((halves,)),
             dma((gz_n,)),
-            dma((layer_n - 1,)),
-            dma((layer_n - 1,)),
-            dma((layer_n - 1,)),
-            dma((layer_n - 1,)),
+            dma((gx_n - 1,)),
+            dma((gx_n - 1,)),
+            dma((gy_n - 1,)),
+            dma((gy_n - 1,)),
+            dma((gy_n - 1,)),
+            dma((gy_n - 1,)),
+            dma((gx_n - 1,)),
+            dma((gx_n - 1,)),
             dma((gz_n,)),
             dma((halves,)),
+            dma((4,)),
         ],
         compiler_params=pltpu.CompilerParams(
             collective_id=0, has_side_effects=True, vmem_limit_bytes=56 * 1024 * 1024
@@ -408,16 +513,42 @@
     )(
         rx,
         ry,
-        scale,
-        live,
+        weights,
+        counts,
         neumann.reshape(subs, inner, inner),
-        schur.reshape(subs, inner, inner),
         basis.reshape(subs, inner, coarse),
-        cmap,
+        coarse_map[:, :, 0],
         inv,
         cbas,
         top_inverse,
     )
+
+    def part_of(shape):
+        block = shape[:-1] + (width,)
+        return pl.BlockSpec(block, lambda k: (0,) * (len(shape) - 1) + (k,))
+
+    def whole(shape):
+        return pl.BlockSpec(shape, lambda k: (0,) * len(shape))
+
+    image_shape = (subs, inner, loads)
+    z_x, z_y, image = pl.pallas_call(
+        image_kernel,
+        grid=(halves,),
+        out_shape=(
+            jax.ShapeDtypeStruct(rx.shape, F32),
+            jax.ShapeDtypeStruct(ry.shape, F32),
+            jax.ShapeDtypeStruct(image_shape, BF16),
+        ),
+        in_specs=[
+            part_of(rx.shape),
+            part_of(ry.shape),
+            whole(counts.shape),
+            whole((subs, inner, inner)),
+        ],
+        out_specs=(part_of(rx.shape), part_of(ry.shape), part_of(image_shape)),
+        compiler_params=pltpu.CompilerParams(vmem_limit_bytes=48 * 1024 * 1024),
+        name="schur_image",
+    )(zx, zy, counts, schur.reshape(subs, inner, inner))
     return (
         z_x[:, :, None],
         z_y[:, :, None],

time: 117 us -> 103 us (0.88)
  the two profiles are of different devices: /device:TPU:0 before, /device:TPU:30 now
where the time goes in v2:
time: 103 us
  Pallas kernels  97.7 us (95%)
  local copies, waits for them, and re-layouts  4.68 us (5%)
    pallas_call x1, Pallas kernels, on_device(): pl.pallas_call(functools.partial(kernel, sizes, owners), out_shape=(jax.S...  94.5 us
    unnamed x9, local copies, waits for them, and re-layouts  4.68 us
    pallas_call x1, Pallas kernels, on_device(): pl.pallas_call(image_kernel, grid=(halves,), out_shape=(jax.ShapeDtypeStr...  3.29 us

profile of v2, /device:TPU:30, one launch (start us, length us, event | category | flops | bytes accessed | tf_op | source)
XLA Modules:
  0.0 103.1 jit_solution(15047346858888731768)
XLA Ops:
  0.6 1.9 %copy.14 = bf16[2,2,1,480,64]{4,3,1,0,2:T(8,128)(2,1)} copy(bf16[2,2,1,480,64]{3,4,2,1,0:T(8,128)(2,1)} %param.17) | data formatting | bytes 491520 | tf_op args[6]
  2.6 0.0 copy-start
  2.6 0.0 copy-start.3
  2.6 94.5 %bddc.1 = (f32[3,2,120,512]{3,2,1,0:T(8,128)}, f32[2,3,120,512]{3,2,1,0:T(8,128)}) custom-call(f32[3,2,120,512]{3,2,1,0:T(8,128)} %bitcast.24, f32[2,3,120,512]{3,2,1,0:T(8,128)} %bitcast.25, f32[2,2,4,120]{3,2,1,0:T(4,128)} %bitcast.28, s32[2,2,4]{2,1,0:T(2,128)} %bitcast.20, bf16[4,480,480]{2,1,0:T(8,128)(2,1)} %bitcast.22, bf16[4,480,64]{2,1,0:T(8,128)(2,1)} %bitcast.23, ...), custom_call_target="tpu_custom_call" | custom-call | tf_op jit(solution)/shard_map/bddc/pallas_call | solution.py:455
  97.0 0.0 copy-done
  97.0 0.0 copy-done.3
  97.1 0.0 copy-start.1
  97.1 1.4 %copy-done.1 = f32[3,2,120,512]{3,2,1,0:T(8,128)S(1)} copy-done((f32[3,2,120,512]{3,2,1,0:T(8,128)S(1)}, f32[3,2,120,512]{3,2,1,0:T(8,128)}, u32[]{:S(2)}) %copy-start.1) | copy-done | bytes 1474584
  98.4 0.0 copy-start.2
  98.4 1.4 %copy-done.2 = f32[2,3,120,512]{3,2,1,0:T(8,128)S(1)} copy-done((f32[2,3,120,512]{3,2,1,0:T(8,128)S(1)}, f32[2,3,120,512]{3,2,1,0:T(8,128)}, u32[]{:S(2)}) %copy-start.2) | copy-done | bytes 1474584
  99.8 3.3 %schur_image.1 = (f32[3,2,120,512]{3,2,1,0:T(8,128)}, f32[2,3,120,512]{3,2,1,0:T(8,128)}, bf16[4,480,512]{2,1,0:T(8,128)(2,1)}) custom-call(f32[3,2,120,512]{3,2,1,0:T(8,128)S(1)} %copy-done.1, f32[2,3,120,512]{3,2,1,0:T(8,128)S(1)} %copy-done.2, s32[2,2,4]{2,1,0:T(2,128)S(1)} %bitcast.21, bf16[4,480,480]{2,1,0:T(8,128)(2,1)S(1)} %bitcast.19), custom_call_target="tpu_custom_call" | custom-call | tf_op jit(solution)/shard_map/schur_image/pallas_call | solution.py:534
Async XLA Ops:
  2.6 94.5 %copy-start = (bf16[2,2,1,480,480]{4,3,2,1,0:T(8,128)(2,1)S(1)}, bf16[2,2,1,480,480]{4,3,2,1,0:T(8,128)(2,1)}, u32[]{:S(2)}) copy-start(bf16[2,2,1,480,480]{4,3,2,1,0:T(8,128)(2,1)} %param.16) | copy-start | bytes 5529604
  2.6 94.5 %copy-start.3 = (s32[2,2,1,4]{3,2,1,0:T(1,128)S(1)}, s32[2,2,1,4]{3,2,1,0:T(1,128)}, u32[]{:S(2)}) copy-start(s32[2,2,1,4]{3,2,1,0:T(1,128)} %param.14) | copy-start | bytes 196
  97.1 1.4 %copy-start.1 = (f32[3,2,120,512]{3,2,1,0:T(8,128)S(1)}, f32[3,2,120,512]{3,2,1,0:T(8,128)}, u32[]{:S(2)}) copy-start(f32[3,2,120,512]{3,2,1,0:T(8,128)} %get-tuple-element.8.zx) | copy-start | bytes 4423684
  98.4 1.4 %copy-start.2 = (f32[2,3,120,512]{3,2,1,0:T(8,128)S(1)}, f32[2,3,120,512]{3,2,1,0:T(8,128)}, u32[]{:S(2)}) copy-start(f32[2,3,120,512]{3,2,1,0:T(8,128)} %get-tuple-element.9.zy) | copy-start | bytes 4423684
